TPU v7x, 32 devices: a whole 2x2x4 slice. The times are simulated.
32 devices in a mesh: ep: 16 (over z, y, x), etp: 2 (over core).
Axes of the slice: x: 2, y: 2, z: 4, core: 2. Of those that a mesh axis runs over, the one named last changes fastest.
Arguments:
- tokens: bfloat16 [1024, 7168], P('ep', 'etp'), may hold values from -6 to 6
- cotangent: bfloat16 [1024, 7168], P('ep', 'etp'), may hold values from -6 to 6
- expert_ids: int32 [1024, 8], P('ep'), may hold values from 0 to 15, all different within a row; in each aligned block of 64 rows (0 to 63, 64 to 127, ...) at most 40 rows name the same one
- routing_gate_weight: bfloat16 [1024, 8], P('ep'), may hold values from 0.049804688 to 1
- gate_projection_weight: bfloat16 [16, 7168, 2048], P('ep', None, 'etp'), may hold values from -0.0625 to 0.0625
- up_weight: bfloat16 [16, 7168, 2048], P('ep', None, 'etp'), may hold values from -0.0625 to 0.0625
- down_weight: bfloat16 [16, 2048, 7168], P('ep', 'etp'), may hold values from -0.125 to 0.125
Outputs:
- input_grad: bfloat16 [1024, 7168], P('ep', 'etp')
- gate_grad: float32 [1024, 8], P('ep')
- w_gate_grad: bfloat16 [16, 7168, 2048], P('ep', None, 'etp')
- w_up_grad: bfloat16 [16, 7168, 2048], P('ep', None, 'etp')
- w_down_grad: bfloat16 [16, 2048, 7168], P('ep', 'etp')
Inputs may be any that keep to these rules, and one draw needn't show every extreme that they name: `expert_ids`: each row names 8 different experts. Among the rows of one index of ep no expert is named more than 40 times, a bound that some block reaches.
All inputs are finite; a program needn't handle non-finite values.
Results may differ from a plain program's by a relative error of at most 0.019.
Values may be sent and summed in bfloat16 or wider, within the bound.
A program may use at most 192 MiB of HBM per device.

v0:
```python
import jax
import jax.numpy as jnp
from jax import lax
from jax.sharding import PartitionSpec as P


def local(
    tokens,
    cotangent,
    expert_ids,
    routing_gate_weight,
    gate_projection_weight,
    up_weight,
    down_weight,
):
    ep_count = lax.axis_size("ep")
    tok_rows = tokens.shape[0]
    choose = expert_ids.shape[1]
    capacity = min(tok_rows, tok_rows * choose * 5 // (4 * ep_count))
    width = down_weight.shape[2]
    flat_ids = expert_ids.reshape(-1)
    onehot = (flat_ids[:, None] == jnp.arange(ep_count, dtype=jnp.int32)[None, :]).astype(jnp.int32)
    before = jnp.cumsum(onehot, axis=0) - onehot
    rank = jnp.sum(before * onehot, axis=1)
    target_slot = flat_ids * capacity + rank
    source = jnp.repeat(jnp.arange(tok_rows, dtype=jnp.int32), choose)
    slot_positions = ep_count * capacity
    slice_cols = tokens.shape[1]
    send_x = (
        jnp.zeros((slot_positions, slice_cols), jnp.bfloat16)
        .at[target_slot]
        .set(tokens[source])
        .reshape(ep_count, capacity, slice_cols)
    )
    send_dy = (
        jnp.zeros((slot_positions, slice_cols), jnp.bfloat16)
        .at[target_slot]
        .set(cotangent[source])
        .reshape(ep_count, capacity, slice_cols)
    )
    send_g = (
        jnp.zeros((slot_positions,), jnp.bfloat16)
        .at[target_slot]
        .set(routing_gate_weight.reshape(-1))
        .reshape(ep_count, capacity)
    )
    recv_x, recv_dy, recv_g = (
        lax.all_to_all(send_x, "ep", split_axis=0, concat_axis=0, tiled=True),
        lax.all_to_all(send_dy, "ep", split_axis=0, concat_axis=0, tiled=True),
        lax.all_to_all(send_g, "ep", split_axis=0, concat_axis=0, tiled=True),
    )
    full_x, full_dy = (
        lax.all_gather(recv_x, "etp", axis=2, tiled=True),
        lax.all_gather(recv_dy, "etp", axis=2, tiled=True),
    )
    xe = full_x.reshape(slot_positions, width)
    dye = full_dy.reshape(slot_positions, width)
    wg = gate_projection_weight[0]
    wu = up_weight[0]
    wd = down_weight[0]
    a = jnp.dot(xe, wg, preferred_element_type=jnp.float32)
    b = jnp.dot(xe, wu, preferred_element_type=jnp.float32)
    sig = jax.nn.sigmoid(a)
    s = a * sig
    h = s * b
    gf = recv_g.reshape(slot_positions).astype(jnp.float32)[:, None]
    hs = (gf * h).astype(jnp.bfloat16)
    down_weight_gradient = jnp.dot(hs.T, dye, preferred_element_type=jnp.float32).astype(
        jnp.bfloat16
    )
    raw = jnp.dot(dye, wd.T, preferred_element_type=jnp.float32)
    gate_local = jnp.sum(h * raw, axis=1)
    dh = gf * raw
    da = (dh * b * sig * (1.0 + a * (1.0 - sig))).astype(jnp.bfloat16)
    db = (dh * s).astype(jnp.bfloat16)
    gate_weight_gradient = jnp.dot(xe.T, da, preferred_element_type=jnp.float32).astype(
        jnp.bfloat16
    )
    up_weight_gradient = jnp.dot(xe.T, db, preferred_element_type=jnp.float32).astype(jnp.bfloat16)
    partial_value = jnp.dot(da, wg.T, preferred_element_type=jnp.float32) + jnp.dot(
        db, wu.T, preferred_element_type=jnp.float32
    )
    rounded = partial_value.astype(jnp.bfloat16)
    slotted_gate = lax.psum(gate_local, "etp").reshape(ep_count, capacity)
    terms = lax.optimization_barrier(rounded).astype(jnp.float32).reshape(ep_count, capacity, width)
    share = lax.psum_scatter(
        terms.astype(jnp.bfloat16), "etp", scatter_dimension=2, tiled=True
    ).astype(jnp.float32)
    back, gate_back = (
        lax.all_to_all(share, "ep", split_axis=0, concat_axis=0, tiled=True),
        lax.all_to_all(slotted_gate, "ep", split_axis=0, concat_axis=0, tiled=True),
    )
    picked = back.reshape(slot_positions, slice_cols)[target_slot].reshape(
        tok_rows, choose, slice_cols
    )
    input_grad = jnp.sum(picked, axis=1).astype(jnp.bfloat16)
    gate_grad = gate_back.reshape(slot_positions)[target_slot].reshape(tok_rows, choose)
    return (
        input_grad,
        gate_grad,
        gate_weight_gradient[None],
        up_weight_gradient[None],
        down_weight_gradient[None],
    )


def solution(mesh):
    in_specs = (
        P("ep", "etp"),
        P("ep", "etp"),
        P("ep", None),
        P("ep", None),
        P("ep", None, "etp"),
        P("ep", None, "etp"),
        P("ep", "etp", None),
    )
    out_specs = (
        P("ep", "etp"),
        P("ep", None),
        P("ep", None, "etp"),
        P("ep", None, "etp"),
        P("ep", "etp", None),
    )
    return jax.shard_map(local, mesh=mesh, in_specs=in_specs, out_specs=out_specs, check_vma=False)
```

profile of v0, /device:TPU:10, one launch (start us, length us, event | category | flops | bytes accessed | tf_op | source)
XLA Modules:
  0.0 624.5 jit_solution(5873178967026368647)
XLA Ops:
  7.2 0.8 copy.19
  8.2 0.7 broadcast_multiply_fusion
  8.9 1.1 reduce-window.6
  10.1 0.2 slice_reduce_fusion
  10.8 19.3 %scatter_custom_fusion.2 = bf16[640,3584]{1,0:T(8,128)(2,1)} fusion(s32[512]{0:T(512)S(1)} %bitcast.66, bf16[64,3584]{1,0:T(8,128)(2,1)S(1)} %copy-done, s32[1024]{0:T(1024)S(1)} %pad_clamp_fusion.1, bf16[]{:T(256)} %constant.7.clone.1), kind=kCustom, calls=%fused_computation.22 | custom fusion | bytes 4587522 | tf_op jit(solution)/shard_map/scatter | solution.py:32
  30.1 108.0 %all_to_all.34 = bf16[16,40,3584]{2,1,0:T(8,128)(2,1)} all-to-all(bf16[16,40,3584]{2,1,0:T(8,128)(2,1)} %bitcast.64), channel_id=1, replica_groups=mesh['ep'=16,'etp'=2] {'ep'}, dimensions={0} | all-to-all | bytes 9175040 | tf_op jit(solution)/shard_map/all_to_all | solution.py:48
  138.1 0.4 all-gather.3.cloned.1.call-start
  138.6 19.3 %scatter_custom_fusion.1 = bf16[640,3584]{1,0:T(8,128)(2,1)} fusion(s32[512]{0:T(512)S(1)} %bitcast.67, bf16[64,3584]{1,0:T(8,128)(2,1)} %param.8, s32[1024]{0:T(1024)S(1)} %pad_clamp_fusion.1, bf16[]{:T(256)} %constant.7.clone.1), kind=kCustom, calls=%fused_computation.24 | custom fusion | bytes 4588032 | tf_op jit(solution)/shard_map/scatter | solution.py:38
  157.9 105.5 %all_to_all.35 = bf16[16,40,3584]{2,1,0:T(8,128)(2,1)} all-to-all(bf16[16,40,3584]{2,1,0:T(8,128)(2,1)} %bitcast.63), channel_id=1, replica_groups=mesh['ep'=16,'etp'=2] {'ep'}, dimensions={0} | all-to-all | bytes 9175040 | tf_op jit(solution)/shard_map/all_to_all | solution.py:49
  263.5 0.6 copy-done.2
  264.3 3.8 scatter_custom_fusion
  268.2 10.4 %all_to_all.36 = bf16[16,1,40]{2,1,0:T(2,128)(2,1)S(1)} all-to-all(bf16[16,1,40]{2,1,0:T(2,128)(2,1)S(1)} %all_to_all.28), channel_id=1, replica_groups=mesh['ep'=16,'etp'=2] {'ep'}, dimensions={0} | all-to-all | bytes 2560 | tf_op jit(solution)/shard_map/all_to_all | solution.py:50
  278.7 14.4 %fusion.2 = f32[640,1024]{1,0:T(8,128)S(1)} fusion(bf16[640,7168]{1,0:T(8,128)(2,1)} %bitcast.72, bf16[1,7168,1024]{2,1,0:T(8,128)(2,1)} %param.11), kind=kOutput, calls=%fused_computation.10 | convolution fusion | flops 9395240960 | bytes 26476544 | tf_op jit(solution)/shard_map/dot_general | solution.py:61
  293.2 14.1 %fusion.6 = f32[640,1024]{1,0:T(8,128)} fusion(bf16[640,7168]{1,0:T(8,128)(2,1)S(1)} %bitcast.74, bf16[1,7168,1024]{2,1,0:T(8,128)(2,1)} %param.12), kind=kOutput, calls=%fused_computation.14 | convolution fusion | flops 9395240960 | bytes 26476544 | tf_op jit(solution)/shard_map/dot_general | solution.py:62
  307.3 17.3 %multiply_reduce_fusion = (f32[640]{0:T(1024)S(1)}, bf16[640,1024]{1,0:T(8,128)(2,1)S(1)}, bf16[640,1024]{1,0:T(8,128)(2,1)S(1)}) fusion(f32[640,1024]{1,0:T(8,128)} %fusion.6, f32[640,1024]{1,0:T(8,128)S(1)} %fusion.2, f32[640]{0:T(1024)S(1)} %reshape.147, bf16[640,7168]{1,0:T(8,128)(2,1)} %bitcast.78, bf16[1,1024,7168]{2,1,0:T(8,128)(2,1)} %param.13), kind=kOutput, calls=%fused_computation.27 | convolution fusion | flops 9406381056 | bytes 31724544 | tf_op jit(solution)/shard_map/dot_general | solution.py:71
  324.6 17.4 %fusion = f32[640,7168]{1,0:T(8,128)} fusion(bf16[640,1024]{1,0:T(8,128)(2,1)S(1)} %get-tuple-element.16, bf16[1,7168,1024]{2,1,0:T(8,128)(2,1)} %param.11), kind=kOutput, calls=%fused_computation.8 | convolution fusion | flops 9395240960 | bytes 34340864 | tf_op jit(solution)/shard_map/dot_general | solution.py:80
  342.0 19.6 %add_convert_fusion = bf16[640,7168]{1,0:T(8,128)(2,1)} fusion(f32[640,7168]{1,0:T(8,128)} %fusion, bf16[640,1024]{1,0:T(8,128)(2,1)S(1)} %get-tuple-element.17, bf16[1,7168,1024]{2,1,0:T(8,128)(2,1)} %param.12), kind=kOutput, calls=%fused_computation.7 | convolution fusion | flops 9404416000 | bytes 43515904 | tf_op jit(solution)/shard_map/dot_general | solution.py:80
  361.8 3.1 psum.7
  364.9 5.9 all-to-all-start.4
  370.7 8.8 %reduce-scatter.2.cloned.1.call-done = bf16[16,40,3584]{2,1,0:T(8,128)(2,1)} async-done(((bf16[16,40,7168]{2,1,0:T(8,128)(2,1)}), bf16[16,40,3584]{2,1,0:T(8,128)(2,1)}) %reduce-scatter.2.cloned.1.call-update) | async-done | bytes 4587536 | tf_op jit(solution)/shard_map/reduce_scatter | solution.py:86
  379.5 7.1 %convert_element_type.57 = f32[16,40,3584]{2,1,0:T(8,128)} convert(bf16[16,40,3584]{2,1,0:T(8,128)(2,1)} %reduce-scatter.2.cloned.1.call-done) | non-fusion elementwise | flops 2293760 | bytes 13762560 | tf_op jit(solution)/shard_map/convert_element_type | solution.py:88
  386.6 7.3 %all-to-all-start.3 = ((f32[16,40,3584]{2,1,0:T(8,128)}), f32[16,40,3584]{2,1,0:T(8,128)}, u32[]{:S(2)}, u32[]{:S(2)}) async-start(f32[16,40,3584]{2,1,0:T(8,128)} %convert_element_type.57), calls=%async_computation.4 | async-start | bytes 18350080 | tf_op jit(solution)/shard_map/all_to_all | solution.py:90
  394.0 18.9 %convert_bitcast_fusion = bf16[1,1024,7168]{2,1,0:T(8,128)(2,1)} fusion(bf16[640,7168]{1,0:T(8,128)(2,1)} %bitcast.79, f32[640]{0:T(1024)S(1)} %reshape.147, f32[640,1024]{1,0:T(8,128)} %fusion.6, f32[640,1024]{1,0:T(8,128)S(1)} %fusion.2), kind=kOutput, calls=%fused_computation.18 | convolution fusion | flops 9407168512 | bytes 29100544 | tf_op jit(solution)/shard_map/dot_general | solution.py:68
  412.8 17.8 %convert_bitcast_fusion.1 = bf16[1,7168,1024]{2,1,0:T(8,128)(2,1)} fusion(bf16[640,7168]{1,0:T(8,128)(2,1)} %bitcast.73, bf16[640,1024]{1,0:T(8,128)(2,1)} %copy-done.6), kind=kOutput, calls=%fused_computation.19 | convolution fusion | flops 9402580992 | bytes 25165824 | tf_op jit(solution)/shard_map/dot_general | solution.py:79
  430.6 14.5 %convert_bitcast_fusion.2 = bf16[1,7168,1024]{2,1,0:T(8,128)(2,1)} fusion(bf16[640,7168]{1,0:T(8,128)(2,1)S(1)} %bitcast.77, bf16[640,1024]{1,0:T(8,128)(2,1)S(1)} %copy-done.5), kind=kOutput, calls=%fused_computation.20 | convolution fusion | flops 9402580992 | bytes 25165824 | tf_op jit(solution)/shard_map/dot_general | solution.py:76
  445.1 0.5 broadcast.111
  445.7 0.7 reduce.9
  446.4 2.3 gather_fusion.1
  448.8 0.7 copy.24
  449.5 150.9 %all-to-all-done.3 = f32[16,40,3584]{2,1,0:T(8,128)} async-done(((f32[16,40,3584]{2,1,0:T(8,128)}), f32[16,40,3584]{2,1,0:T(8,128)}, u32[]{:S(2)}, u32[]{:S(2)}) %all-to-all-start.3) | async-done | bytes 9175072 | tf_op jit(solution)/shard_map/all_to_all | solution.py:90
  600.3 11.8 %gather_fusion = f32[512,3584]{1,0:T(8,128)} fusion(f32[640,3584]{1,0:T(8,128)} %bitcast.12, s32[1024]{0:T(1024)S(1)} %pad_clamp_fusion), kind=kCustom, calls=%fused_computation.2 | custom fusion | bytes 14682112 | tf_op jit(solution)/shard_map/gather | solution.py:93
  612.1 5.6 bitcast_reduce_fusion
  (50 shorter events, 1.5 us)
Async XLA Ops:
  7.2 3.6 copy-start
  7.2 271.5 %all-gather.5.cloned.1.call-start = ((), (), s32[]{:S(2)}) async-start(), calls=%async_computation.7 | async-start | bytes 13762560 | tf_op jit(solution)/shard_map/all_gather | solution.py:53
  138.1 169.1 %all-gather.3.cloned.1.call-start = ((), (), s32[]{:S(2)}) async-start(), calls=%async_computation.6 | async-start | bytes 13762560 | tf_op jit(solution)/shard_map/all_gather | solution.py:54
  263.4 0.7 copy-start.2
  263.4 116.1 %reduce-scatter.2.cloned.1.call-start = ((), (), s32[]{:S(2)}) async-start(), calls=%async_computation.8 | async-start | bytes 13762560 | tf_op jit(solution)/shard_map/reduce_scatter | solution.py:86
  278.7 14.5 %copy-start.3 = (bf16[16,40,7168]{2,1,0:T(8,128)(2,1)S(1)}, bf16[16,40,7168]{2,1,0:T(8,128)(2,1)}, u32[]{:S(2)}) copy-start(bf16[16,40,7168]{2,1,0:T(8,128)(2,1)} %all-gather.5.cloned.1.call-done) | copy-start | bytes 27525124
  324.6 17.4 %copy-start.4 = (bf16[640,1024]{1,0:T(8,128)(2,1)}, bf16[640,1024]{1,0:T(8,128)(2,1)S(1)}, u32[]{:S(2)}) copy-start(bf16[640,1024]{1,0:T(8,128)(2,1)S(1)} %get-tuple-element.16) | copy-start | bytes 3932164
  324.6 17.4 %copy-start.6 = (bf16[640,1024]{1,0:T(8,128)(2,1)}, bf16[640,1024]{1,0:T(8,128)(2,1)S(1)}, u32[]{:S(2)}) copy-start(bf16[640,1024]{1,0:T(8,128)(2,1)S(1)} %get-tuple-element.17) | copy-start | bytes 3932164
  364.9 21.8 %all-to-all-start.4 = ((f32[16,1,40]{2,1,0:T(1,128)}), f32[16,1,40]{2,1,0:T(1,128)S(1)}, u32[]{:S(2)}, u32[]{:S(2)}) async-start(f32[16,1,40]{2,1,0:T(1,128)} %psum.7), calls=%async_computation.5 | async-start | bytes 16384 | tf_op jit(solution)/shard_map/all_to_all | solution.py:91
  386.6 213.7 %all-to-all-start.3 = ((f32[16,40,3584]{2,1,0:T(8,128)}), f32[16,40,3584]{2,1,0:T(8,128)}, u32[]{:S(2)}, u32[]{:S(2)}) async-start(f32[16,40,3584]{2,1,0:T(8,128)} %convert_element_type.57), calls=%async_computation.4 | async-start | bytes 18350080 | tf_op jit(solution)/shard_map/all_to_all | solution.py:90
  393.9 36.7 %slice-start = ((s8[9175040]{0:T(1024)(128)(4,1)}), s8[786432]{0:T(1024)(128)(4,1)S(1)}, s32[]{:S(2)}) async-start(s8[9175040]{0:T(1024)(128)(4,1)} %bitcast.75), calls=%async_computation.9 | async-start | bytes 1572864
  393.9 36.7 %slice-start.1 = ((s8[9175040]{0:T(1024)(128)(4,1)}), s8[4194304]{0:T(1024)(128)(4,1)S(1)}, s32[]{:S(2)}) async-start(s8[9175040]{0:T(1024)(128)(4,1)} %bitcast.75), calls=%async_computation.10 | async-start | bytes 8388608
  412.8 17.8 %slice-start.2 = ((s8[9175040]{0:T(1024)(128)(4,1)}), s8[4194304]{0:T(1024)(128)(4,1)S(1)}, s32[]{:S(2)}) async-start(s8[9175040]{0:T(1024)(128)(4,1)} %bitcast.75), calls=%async_computation.11 | async-start | bytes 8388608
  412.8 17.8 %copy-start.5 = (bf16[640,1024]{1,0:T(8,128)(2,1)S(1)}, bf16[640,1024]{1,0:T(8,128)(2,1)}, u32[]{:S(2)}) copy-start(bf16[640,1024]{1,0:T(8,128)(2,1)} %copy-done.4) | copy-start | bytes 3932164
  600.3 17.4 %copy-start.1 = (bf16[64,3584]{1,0:T(8,128)(2,1)S(1)}, bf16[64,3584]{1,0:T(8,128)(2,1)}, u32[]{:S(2)}) copy-start(bf16[64,3584]{1,0:T(8,128)(2,1)} %param.7) | copy-start | bytes 1376260
Sparse Core Ops, SparseCore 0:
  138.2 21.1 all-gather.4
  263.5 21.1 all-gather.2
  361.8 17.6 reduce-scatter.1
where the time goes:
time: 636 us; the launch traced here: 625 us
  blocking collectives  227 us (36%)
  waiting for transfers between devices  160 us (25%)
  matrix products  134 us (21%)
  local copies, waits for them, and re-layouts  60.4 us (9%)
  other arithmetic  15.4 us (2%)
  between operations  14.2 us (2%)
  starting transfers between devices  13.7 us (2%)
    all_to_all x1, waiting for transfers between devices, local(): lax.all_to_all(share, 'ep', split_axis=0, concat_axis=0, tiled=True)  151 us
    all_to_all x1, blocking collectives, local(): lax.all_to_all(send_x, 'ep', split_axis=0, concat_axis=0, tiled=True)  108 us
    all_to_all x1, blocking collectives, local(): lax.all_to_all(send_dy, 'ep', split_axis=0, concat_axis=0, tiled=True)  105 us
    dot_general x1, matrix products, local(): jnp.dot(db, wu.T, preferred_element_type=jnp.float32)  19.6 us
    scatter x1, local copies, waits for them, and re-layouts, local(): send_dy = jnp.zeros((slot_positions, slice_cols), jnp.bfloat16).at[target...  19.3 us
    scatter x1, local copies, waits for them, and re-layouts, local(): send_x = jnp.zeros((slot_positions, slice_cols), jnp.bfloat16).at[target_...  19.3 us
    dot_general x1, matrix products, local(): jnp.dot(hs.T, dye, preferred_element_type=jnp.float32).astype(jnp.bfloat16)  18.9 us
    dot_general x1, matrix products, local(): jnp.dot(xe.T, db, preferred_element_type=jnp.float32).astype(jnp.bfloat16)  17.8 us
  transfers between devices with their start and end apart: 5, of which 2 were waited for; matrix products, arithmetic and copies ran while one was open for 18% of the time, Pallas kernels for 0%

commit v1 on v0

v1 whole, which is shorter than its diff:
```python
import math

import jax
import jax.numpy as jnp
from jax import lax
from jax.sharding import PartitionSpec as P

F32 = jnp.float32
BF16 = jnp.bfloat16


def local(
    tokens,
    cotangent,
    expert_ids,
    routing_gate_weight,
    gate_projection_weight,
    up_weight,
    down_weight,
):
    ep_count = lax.axis_size("ep")
    me = lax.axis_index("ep")
    rows, cols = tokens.shape
    choose = expert_ids.shape[1]
    capacity = min(rows, rows * choose * 5 // (4 * ep_count))
    total_rows = ep_count * rows
    slots = ep_count * capacity
    per = math.gcd(max(1, 256 // rows), ep_count)
    groups = ep_count // per

    routes = jnp.concatenate(
        [expert_ids.astype(F32), routing_gate_weight.astype(F32)], axis=1
    )
    routes = lax.all_gather(routes, "ep", axis=0, tiled=True)
    x_all = lax.all_gather(tokens, "ep", axis=0, tiled=True)
    x_all, cotangent = lax.optimization_barrier((x_all, cotangent))
    dy_all = lax.all_gather(cotangent, "ep", axis=0, tiled=True)

    hit = routes[:, :choose] == me.astype(F32)
    gate = jnp.sum(jnp.where(hit, routes[:, choose:], 0.0), axis=1)
    named = jnp.any(hit, axis=1).reshape(ep_count, rows)
    rank = jnp.cumsum(named.astype(jnp.int32), axis=1) - 1
    place = rank + (jnp.arange(ep_count, dtype=jnp.int32) % per)[:, None] * capacity
    place = jnp.where(named, place, -1).reshape(groups, 1, per * rows)
    pick = place == jnp.arange(per * capacity, dtype=jnp.int32)[None, :, None]
    select = pick.astype(BF16)
    gf = jnp.sum(jnp.where(pick, gate.reshape(groups, 1, per * rows), 0.0), axis=2)
    gf = gf.reshape(slots, 1)

    def dispatch(all_rows):
        out = jnp.einsum(
            "gst,gtc->gsc",
            select,
            all_rows.reshape(groups, per * rows, cols),
            preferred_element_type=F32,
        )
        out = out.astype(BF16).reshape(slots, cols)
        return lax.all_gather(out, "etp", axis=1, tiled=True)

    wg = gate_projection_weight[0]
    wu = up_weight[0]
    wd = down_weight[0]
    xe = dispatch(x_all)
    a = jnp.dot(xe, wg, preferred_element_type=F32)
    b = jnp.dot(xe, wu, preferred_element_type=F32)
    dye = dispatch(dy_all)
    raw = jnp.dot(dye, wd.T, preferred_element_type=F32)
    sig = jax.nn.sigmoid(a)
    s = a * sig
    h = s * b
    hs = (gf * h).astype(BF16)
    gate_local = jnp.sum(h * raw, axis=1)
    dh = gf * raw
    da = (dh * b * sig * (1.0 + a * (1.0 - sig))).astype(BF16)
    db = (dh * s).astype(BF16)
    partial_value = jnp.dot(da, wg.T, preferred_element_type=F32) + jnp.dot(
        db, wu.T, preferred_element_type=F32
    )
    share = lax.psum_scatter(
        partial_value.astype(BF16), "etp", scatter_dimension=1, tiled=True
    )
    dense = jnp.einsum(
        "gst,gsc->gtc",
        select,
        share.reshape(groups, per * capacity, cols),
        preferred_element_type=F32,
    )
    dense = dense.astype(BF16).reshape(total_rows, cols)
    input_grad = lax.psum_scatter(dense, "ep", scatter_dimension=0, tiled=True)

    gate_rows = jnp.sum(
        jnp.where(pick, gate_local.reshape(groups, per * capacity, 1), 0.0), axis=1
    )
    gate_rows = lax.psum(gate_rows.reshape(ep_count, rows), "etp")
    gate_back = lax.all_to_all(gate_rows, "ep", split_axis=0, concat_axis=0, tiled=True)
    wanted = expert_ids[:, :, None] == jnp.arange(ep_count, dtype=jnp.int32)[None, None, :]
    gate_grad = jnp.sum(jnp.where(wanted, gate_back.T[:, None, :], 0.0), axis=2)

    down_weight_gradient = jnp.dot(hs.T, dye, preferred_element_type=F32).astype(BF16)
    gate_weight_gradient = jnp.dot(xe.T, da, preferred_element_type=F32).astype(BF16)
    up_weight_gradient = jnp.dot(xe.T, db, preferred_element_type=F32).astype(BF16)
    return (
        input_grad,
        gate_grad,
        gate_weight_gradient[None],
        up_weight_gradient[None],
        down_weight_gradient[None],
    )


def solution(mesh):
    in_specs = (
        P("ep", "etp"),
        P("ep", "etp"),
        P("ep", None),
        P("ep", None),
        P("ep", None, "etp"),
        P("ep", None, "etp"),
        P("ep", "etp", None),
    )
    out_specs = (
        P("ep", "etp"),
        P("ep", None),
        P("ep", None, "etp"),
        P("ep", None, "etp"),
        P("ep", "etp", None),
    )
    return jax.shard_map(local, mesh=mesh, in_specs=in_specs, out_specs=out_specs, check_vma=False)
```

time: 636 us -> 528 us (0.83); the launches traced: 625 us -> 524 us
  blocking collectives: 227 us -> 34.7 us
  waiting for transfers between devices: 160 us -> 301 us
  local copies, waits for them, and re-layouts: 60.4 us -> 0.74 us
  matrix products: 134 us -> 159 us
  other arithmetic: 15.4 us -> 6.77 us
    all_to_all x3 -> x0, blocking collectives: 224 us -> none  [the longest x1 108 us: local(): lax.all_to_all(send_x, 'ep', split_axis=0, concat_axis=0, tiled=True)]
    all_gather x2 -> x4, waiting for transfers between devices: 0.02 us -> 187 us  [the longest x1 106 us: local(): x_all = lax.all_gather(tokens, 'ep', axis=0, tiled=True)]
    all_to_all x2 -> x1, waiting for transfers between devices: 151 us -> 0.01 us  [local(): lax.all_to_all(gate_rows, 'ep', split_axis=0, concat_axis=0, tiled=True)]
    reduce_scatter x1 -> x2, waiting for transfers between devices: 8.79 us -> 114 us  [the longest x1 95 us: local(): input_grad = lax.psum_scatter(dense, 'ep', scatter_dimension=0, tiled=True)]
    scatter x3 -> x0, local copies, waits for them, and re-layouts: 42.4 us -> none  [the longest x1 19.3 us: local(): send_dy = jnp.zeros((slot_positions, slice_cols), jnp.bfloat16).at[target...]
    all_gather x0 -> x1, blocking collectives: none -> 31.7 us  [local(): routes = lax.all_gather(routes, 'ep', axis=0, tiled=True)]
    dot_general x8 -> x11, matrix products: 134 us -> 159 us  [the longest x1 19.6 us: local(): jnp.dot(db, wu.T, preferred_element_type=F32)]
    gather x2 -> x0, local copies, waits for them, and re-layouts: 14.1 us -> none  [the longest x1 11.8 us: local(): back.reshape(slot_positions, slice_cols)[target_slot]]
  transfers between devices with their start and end apart: 5 -> 7, of which waited for: 2 -> 5; matrix products, arithmetic and copies ran while one was open for 18% -> 19% of each run, Pallas kernels for 0% -> 0%
where the time goes in v1:
time: 528 us; the launch traced here: 524 us
  waiting for transfers between devices  301 us (57%)
  matrix products  159 us (30%)
  blocking collectives  34.7 us (7%)
  between operations  14.4 us (3%)
  starting transfers between devices  7.97 us (2%)
  other arithmetic  6.77 us (1%)
    all_gather x1, waiting for transfers between devices, local(): x_all = lax.all_gather(tokens, 'ep', axis=0, tiled=True)  106 us
    reduce_scatter x1, waiting for transfers between devices, local(): input_grad = lax.psum_scatter(dense, 'ep', scatter_dimension=0, tiled=True)  95 us
    all_gather x1, waiting for transfers between devices, local(): dy_all = lax.all_gather(cotangent, 'ep', axis=0, tiled=True)  64.1 us
    all_gather x1, blocking collectives, local(): routes = lax.all_gather(routes, 'ep', axis=0, tiled=True)  31.7 us
    dot_general x1, matrix products, local(): jnp.dot(db, wu.T, preferred_element_type=F32)  19.6 us
    reduce_scatter x1, waiting for transfers between devices, local(): lax.psum_scatter(partial_value.astype(BF16), 'etp', scatter_dimension=1,...  18.9 us
    dot_general x1, matrix products, local(): jnp.dot(hs.T, dye, preferred_element_type=F32).astype(BF16)  18.4 us
    dot_general x1, matrix products, local(): jnp.dot(xe.T, db, preferred_element_type=F32).astype(BF16)  18.1 us
  transfers between devices with their start and end apart: 7, of which 5 were waited for; matrix products, arithmetic and copies ran while one was open for 19% of the time, Pallas kernels for 0%

profile of v1, /device:TPU:10, one launch (start us, length us, event | category | flops | bytes accessed | tf_op | source)
XLA Modules:
  0.0 524.4 jit_solution(5282987204771764942)
XLA Ops:
  7.2 0.7 all-gather.6.cloned.1.call-update
  7.9 106.4 %all-gather.6.cloned.1.call-done = bf16[1024,3584]{1,0:T(8,128)(2,1)} async-done(((bf16[64,3584]{1,0:T(8,128)(2,1)}), bf16[1024,3584]{1,0:T(8,128)(2,1)}) %all-gather.6.cloned.1.call-update) | async-done | bytes 7340048 | tf_op jit(solution)/shard_map/all_gather | solution.py:35
  114.4 0.7 convert_element_type.47
  115.1 0.7 convert_element_type.46
  115.8 31.7 %all-gather = f32[16,64,16]{1,2,0:T(8,128)S(1)} all-gather(f32[1,64,16]{1,2,0:T(8,128)S(1)} %maximum_bitcast_fusion), channel_id=1, replica_groups=mesh['ep'=16,'etp'=2] {'ep'}, dimensions={0}, use_global_device_ids=true | all-gather | bytes 69632 | tf_op jit(solution)/shard_map/all_gather | solution.py:34
  147.5 0.1 reshape.91
  147.8 0.2 reduce_window_sum.11
  148.0 0.1 sub.10
  148.2 0.1 add.48
  148.3 6.6 %convolution_convert_fusion.1 = bf16[4,160,3584]{2,1,0:T(8,128)(2,1)} fusion(bf16[4,256,3584]{2,1,0:T(8,128)(2,1)} %bitcast.55, s32[4,256]{1,0:T(4,128)S(1)} %add_select_fusion), kind=kOutput, calls=%fused_computation.15 | convolution fusion | flops 1176862720 | bytes 11931648 | tf_op jit(solution)/shard_map/gst,gtc->gsc/dot_general | solution.py:51
  155.0 64.1 %all-gather.8.cloned.1.call-done = bf16[1024,3584]{1,0:T(8,128)(2,1)} async-done(((bf16[64,3584]{1,0:T(8,128)(2,1)}), bf16[1024,3584]{1,0:T(8,128)(2,1)}) %all-gather.8.cloned.1.call-update) | async-done | bytes 7340048 | tf_op jit(solution)/shard_map/all_gather | solution.py:37
  219.1 6.6 %convolution_convert_fusion.2 = bf16[4,160,3584]{2,1,0:T(8,128)(2,1)} fusion(bf16[4,256,3584]{2,1,0:T(8,128)(2,1)} %bitcast.54, s32[4,256]{1,0:T(4,128)S(1)} %add_select_fusion), kind=kOutput, calls=%fused_computation.16 | convolution fusion | flops 1176862720 | bytes 11931648 | tf_op jit(solution)/shard_map/gst,gtc->gsc/dot_general | solution.py:51
  225.7 0.5 reduce-scatter.3.cloned.1.call-start
  226.2 16.0 %all-gather.12.cloned.1.call-done = bf16[640,7168]{1,0:T(8,128)(2,1)} async-done(((bf16[640,3584]{1,0:T(8,128)(2,1)}), bf16[640,7168]{1,0:T(8,128)(2,1)}) %all-gather.12.cloned.1.call-update) | async-done | bytes 9175056 | tf_op jit(solution)/shard_map/all_gather | solution.py:58
  242.2 14.5 %fusion.6 = f32[640,1024]{1,0:T(8,128)S(1)} fusion(bf16[640,7168]{1,0:T(8,128)(2,1)} %all-gather.12.cloned.1.call-done, bf16[1,7168,1024]{2,1,0:T(8,128)(2,1)} %param.12), kind=kOutput, calls=%fused_computation.7 | convolution fusion | flops 9395240960 | bytes 26476544 | tf_op jit(solution)/shard_map/dot_general | solution.py:65
  256.7 14.6 %fusion.2 = f32[640,1024]{1,0:T(8,128)} fusion(bf16[640,7168]{1,0:T(8,128)(2,1)S(1)} %copy-done.5, bf16[1,7168,1024]{2,1,0:T(8,128)(2,1)} %param.11), kind=kOutput, calls=%fused_computation.3 | convolution fusion | flops 9395240960 | bytes 26476544 | tf_op jit(solution)/shard_map/dot_general | solution.py:64
  271.3 17.5 %multiply_reduce_fusion = (f32[640]{0:T(1024)S(1)}, f32[640,1024]{1,0:T(8,128)}) fusion(f32[640,1024]{1,0:T(8,128)S(1)} %fusion.6, f32[640,1024]{1,0:T(8,128)} %fusion.2, bf16[640,7168]{1,0:T(8,128)(2,1)} %all-gather.10.cloned.1.call-done, bf16[1,1024,7168]{2,1,0:T(8,128)(2,1)} %param.13), kind=kOutput, calls=%fused_computation.18 | convolution fusion | flops 9399827456 | bytes 31721984 | tf_op jit(solution)/shard_map/dot_general | solution.py:67
  288.8 0.1 broadcast_in_dim.62
  288.9 0.4 select_reduce_fusion
  289.3 0.1 mul.49
  289.4 4.1 multiply_convert_fusion.1
  293.5 17.4 %fusion = f32[640,7168]{1,0:T(8,128)} fusion(bf16[640,1024]{1,0:T(8,128)(2,1)S(1)} %get-tuple-element.14, bf16[1,7168,1024]{2,1,0:T(8,128)(2,1)} %param.11), kind=kOutput, calls=%fused_computation.1 | convolution fusion | flops 9395240960 | bytes 34340864 | tf_op jit(solution)/shard_map/dot_general | solution.py:76
  311.0 19.6 %add_convert_fusion = bf16[640,7168]{1,0:T(8,128)(2,1)} fusion(f32[640,7168]{1,0:T(8,128)} %fusion, bf16[640,1024]{1,0:T(8,128)(2,1)S(1)} %get-tuple-element.13, bf16[1,7168,1024]{2,1,0:T(8,128)(2,1)} %param.12), kind=kOutput, calls=%fused_computation | convolution fusion | flops 9404416000 | bytes 43515904 | tf_op jit(solution)/shard_map/dot_general | solution.py:76
  330.6 18.9 %reduce-scatter.3.cloned.1.call-done = bf16[640,3584]{1,0:T(8,128)(2,1)} async-done(((bf16[640,7168]{1,0:T(8,128)(2,1)}), bf16[640,3584]{1,0:T(8,128)(2,1)}) %reduce-scatter.3.cloned.1.call-update) | async-done | bytes 4587536 | tf_op jit(solution)/shard_map/reduce_scatter | solution.py:79
  349.6 7.4 %convolution_convert_fusion = bf16[4,256,3584]{2,1,0:T(8,128)(2,1)} fusion(bf16[4,160,3584]{2,1,0:T(8,128)(2,1)} %bitcast.53, s32[4,256]{1,0:T(4,128)S(1)} %add_select_fusion), kind=kOutput, calls=%fused_computation.14 | convolution fusion | flops 1178238976 | bytes 11931648 | tf_op jit(solution)/shard_map/gst,gsc->gtc/dot_general | solution.py:82
  357.1 3.0 psum.7
  360.1 7.3 %all-to-all-start = ((f32[16,1,64]{2,1,0:T(1,128)}), f32[16,1,64]{2,1,0:T(1,128)S(1)}, u32[]{:S(2)}, u32[]{:S(2)}) async-start(f32[16,1,64]{2,1,0:T(1,128)} %bitcast.10), calls=%async_computation.2 | async-start | bytes 16384 | tf_op jit(solution)/shard_map/all_to_all | solution.py:95
  367.4 17.7 %convert_bitcast_fusion.2 = bf16[1,7168,1024]{2,1,0:T(8,128)(2,1)} fusion(bf16[640,7168]{1,0:T(8,128)(2,1)} %all-gather.12.cloned.1.call-done, bf16[640,1024]{1,0:T(8,128)(2,1)} %copy-done.3), kind=kOutput, calls=%fused_computation.13 | convolution fusion | flops 9402580992 | bytes 25165824 | tf_op jit(solution)/shard_map/dot_general | solution.py:100
  385.1 18.1 %convert_bitcast_fusion.1 = bf16[1,7168,1024]{2,1,0:T(8,128)(2,1)} fusion(bf16[640,7168]{1,0:T(8,128)(2,1)} %all-gather.12.cloned.1.call-done, bf16[640,1024]{1,0:T(8,128)(2,1)S(1)} %copy-done.2), kind=kOutput, calls=%fused_computation.12 | convolution fusion | flops 9402580992 | bytes 25165824 | tf_op jit(solution)/shard_map/dot_general | solution.py:101
  403.3 18.4 %convert_bitcast_fusion = bf16[1,1024,7168]{2,1,0:T(8,128)(2,1)} fusion(bf16[640,7168]{1,0:T(8,128)(2,1)} %all-gather.10.cloned.1.call-done, f32[640]{0:T(1024)S(1)} %mul.49, f32[640,1024]{1,0:T(8,128)S(1)} %fusion.6, f32[640,1024]{1,0:T(8,128)S(1)} %copy-done), kind=kOutput, calls=%fused_computation.11 | convolution fusion | flops 9407168512 | bytes 29100544 | tf_op jit(solution)/shard_map/dot_general | solution.py:99
  421.7 0.6 select_reduce_fusion.2
  422.3 95.0 %reduce-scatter.5.cloned.1.call-done = bf16[64,3584]{1,0:T(8,128)(2,1)} async-done(((bf16[1024,3584]{1,0:T(8,128)(2,1)}), bf16[64,3584]{1,0:T(8,128)(2,1)}) %reduce-scatter.5.cloned.1.call-update) | async-done | bytes 458768 | tf_op jit(solution)/shard_map/reduce_scatter | solution.py:89
  (37 shorter events, 0.7 us)
Async XLA Ops:
  7.2 107.2 %all-gather.6.cloned.1.call-start = ((), (), s32[]{:S(2)}) async-start(), calls=%async_computation.3 | async-start | bytes 7798784 | tf_op jit(solution)/shard_map/all_gather | solution.py:35
  7.9 211.2 %all-gather.8.cloned.1.call-start = ((), (), s32[]{:S(2)}) async-start(), calls=%async_computation.4 | async-start | bytes 7798784 | tf_op jit(solution)/shard_map/all_gather | solution.py:37
  114.4 127.9 %all-gather.12.cloned.1.call-start = ((), (), s32[]{:S(2)}) async-start(), calls=%async_computation.6 | async-start | bytes 13762560 | tf_op jit(solution)/shard_map/all_gather | solution.py:58
  154.9 116.4 %all-gather.10.cloned.1.call-start = ((), (), s32[]{:S(2)}) async-start(), calls=%async_computation.5 | async-start | bytes 13762560 | tf_op jit(solution)/shard_map/all_gather | solution.py:58
  225.7 123.9 %reduce-scatter.3.cloned.1.call-start = ((), (), s32[]{:S(2)}) async-start(), calls=%async_computation.7 | async-start | bytes 13762560 | tf_op jit(solution)/shard_map/reduce_scatter | solution.py:79
  242.2 14.5 %copy-start.5 = (bf16[640,7168]{1,0:T(8,128)(2,1)S(1)}, bf16[640,7168]{1,0:T(8,128)(2,1)}, u32[]{:S(2)}) copy-start(bf16[640,7168]{1,0:T(8,128)(2,1)} %all-gather.12.cloned.1.call-done) | copy-start | bytes 27525124
  293.5 17.5 %copy-start.3 = (bf16[640,1024]{1,0:T(8,128)(2,1)}, bf16[640,1024]{1,0:T(8,128)(2,1)S(1)}, u32[]{:S(2)}) copy-start(bf16[640,1024]{1,0:T(8,128)(2,1)S(1)} %get-tuple-element.14) | copy-start | bytes 3932164
  293.5 17.5 %copy-start.1 = (bf16[640,1024]{1,0:T(8,128)(2,1)}, bf16[640,1024]{1,0:T(8,128)(2,1)S(1)}, u32[]{:S(2)}) copy-start(bf16[640,1024]{1,0:T(8,128)(2,1)S(1)} %get-tuple-element.13) | copy-start | bytes 3932164
  330.6 186.7 %reduce-scatter.5.cloned.1.call-start = ((), (), s32[]{:S(2)}) async-start(), calls=%async_computation.8 | async-start | bytes 7798784 | tf_op jit(solution)/shard_map/reduce_scatter | solution.py:89
  360.1 61.6 %all-to-all-start = ((f32[16,1,64]{2,1,0:T(1,128)}), f32[16,1,64]{2,1,0:T(1,128)S(1)}, u32[]{:S(2)}, u32[]{:S(2)}) async-start(f32[16,1,64]{2,1,0:T(1,128)} %bitcast.10), calls=%async_computation.2 | async-start | bytes 16384 | tf_op jit(solution)/shard_map/all_to_all | solution.py:95
  367.4 17.7 %copy-start.2 = (bf16[640,1024]{1,0:T(8,128)(2,1)S(1)}, bf16[640,1024]{1,0:T(8,128)(2,1)}, u32[]{:S(2)}) copy-start(bf16[640,1024]{1,0:T(8,128)(2,1)} %copy-done.1) | copy-start | bytes 3932164
  385.1 18.1 %copy-start = (f32[640,1024]{1,0:T(8,128)S(1)}, f32[640,1024]{1,0:T(8,128)}, u32[]{:S(2)}) copy-start(f32[640,1024]{1,0:T(8,128)} %fusion.2) | copy-start | bytes 7864324
  403.3 18.4 %copy-start.4 = (s32[64,8]{0,1:T(8,128)S(1)}, s32[64,8]{0,1:T(8,128)}, u32[]{:S(2)}) copy-start(s32[64,8]{0,1:T(8,128)} %param.9) | copy-start | bytes 6148
Sparse Core Ops, SparseCore 0:
  10.7 103.6 all-gather.5
  117.0 101.9 all-gather.7
  221.2 20.9 all-gather.11
  244.2 22.7 all-gather.9
  330.7 18.8 reduce-scatter.2
  357.1 160.1 reduce-scatter.4

commit v2 on v1

v2 whole, which is shorter than its diff:
```python
import math

import jax
import jax.numpy as jnp
from jax import lax
from jax.sharding import PartitionSpec as P

F32 = jnp.float32
BF16 = jnp.bfloat16


OFFSETS = (0, 1, -1, 2)


def shift(value, offset):
    n = lax.axis_size("ep")
    return lax.ppermute(value, "ep", [(i, (i + 4 * offset) % n) for i in range(n)])


def swap(value, bits):
    n = lax.axis_size("ep")
    return lax.ppermute(value, "ep", [(i, i ^ bits) for i in range(n)])


def swap_core(value):
    return lax.ppermute(value, "etp", [(0, 1), (1, 0)])


def spread_plane(value):
    half = value.shape[1] // 2
    by_x = swap(value, 1)
    by_y = swap(value, 2)
    lower = swap(by_y[:, :half], 1)
    upper = swap(by_x[:, half:], 2)
    return by_x, by_y, lower, upper


def gather_planes(block, after=None):
    if after is not None:
        block = lax.optimization_barrier((block,) + tuple(after))[0]
    far = [shift(block, -offset) for offset in OFFSETS[1:]]
    near = jnp.stack(far[:2])
    planes = []
    for batch in (block[None], near, far[2][None]):
        by_x, by_y, lower, upper = spread_plane(batch)
        for k in range(batch.shape[0]):
            planes.append(
                jnp.concatenate([batch[k], by_x[k], by_y[k], lower[k], upper[k]], axis=0)
            )
    return planes, far


def reduce_planes(dense):
    half = dense.shape[2] // 2
    from_x = swap(dense[:, 3, :half], 1)
    from_y = swap(dense[:, 3, half:], 2)
    for_y = jnp.concatenate(
        [
            (dense[:, 2, :half].astype(F32) + from_x.astype(F32)).astype(BF16),
            dense[:, 2, half:],
        ],
        axis=1,
    )
    for_x = jnp.concatenate(
        [
            dense[:, 1, :half],
            (dense[:, 1, half:].astype(F32) + from_y.astype(F32)).astype(BF16),
        ],
        axis=1,
    )
    got_y = swap(for_y, 2)
    got_x = swap(for_x, 1)
    total = (dense[:, 0].astype(F32) + got_x.astype(F32) + got_y.astype(F32)).astype(BF16)
    result = total[0].astype(F32)
    for k in range(1, 4):
        result = result + shift(total[k], OFFSETS[k]).astype(F32)
    return result.astype(BF16)


def local(
    tokens,
    cotangent,
    expert_ids,
    routing_gate_weight,
    gate_projection_weight,
    up_weight,
    down_weight,
):
    ep_count = lax.axis_size("ep")
    me = lax.axis_index("ep")
    core = lax.axis_index("etp")
    rows, cols = tokens.shape
    choose = expert_ids.shape[1]
    capacity = min(rows, rows * choose * 5 // (4 * ep_count))
    slots = ep_count * capacity
    pair = lax.axis_size("etp") == 2
    stepwise = ep_count == 16 and pair
    per = 4 if stepwise else math.gcd(max(1, 256 // rows), ep_count)
    groups = ep_count // per

    pad = -2 * choose % 128
    block = jnp.concatenate(
        [
            tokens,
            expert_ids.astype(BF16),
            routing_gate_weight,
            jnp.zeros((rows, pad), BF16),
        ],
        axis=1,
    )
    if stepwise:
        x_groups, far = gather_planes(block)
        dy_groups, _ = gather_planes(cotangent, far)
        offsets = jnp.asarray(OFFSETS, jnp.int32)[:, None]
        places = jnp.arange(4, dtype=jnp.int32)[None, :]
        blocks = ((me // 4 + offsets) % 4 * 4 + (me % 4 ^ places)).reshape(-1)
    else:
        x_all = lax.all_gather(block, "ep", axis=0, tiled=True)
        dy_all = lax.all_gather(cotangent, "ep", axis=0, tiled=True)
        x_groups = list(x_all.reshape(groups, per * rows, -1))
        dy_groups = list(dy_all.reshape(groups, per * rows, -1))
        blocks = jnp.arange(ep_count, dtype=jnp.int32)

    routes = jnp.concatenate([g[:, cols : cols + 2 * choose] for g in x_groups], axis=0)
    routes = routes.astype(F32)
    hit = routes[:, :choose] == me.astype(F32)
    gate = jnp.sum(jnp.where(hit, routes[:, choose:], 0.0), axis=1)
    named = jnp.any(hit, axis=1).reshape(ep_count, rows)
    rank = jnp.cumsum(named.astype(jnp.int32), axis=1) - 1
    place = rank + (jnp.arange(ep_count, dtype=jnp.int32) % per)[:, None] * capacity
    place = jnp.where(named, place, -1).reshape(groups, 1, per * rows)
    pick = place == jnp.arange(per * capacity, dtype=jnp.int32)[None, :, None]
    select = pick.astype(BF16)
    gf = jnp.sum(jnp.where(pick, gate.reshape(groups, 1, per * rows), 0.0), axis=2)
    gf = gf.reshape(slots, 1)

    def dispatch(parts):
        return jnp.concatenate(
            [
                jnp.dot(select[i], part[:, :cols], preferred_element_type=F32).astype(BF16)
                for i, part in enumerate(parts)
            ],
            axis=0,
        )

    wg = gate_projection_weight[0]
    wu = up_weight[0]
    wd = down_weight[0]
    xe = lax.all_gather(dispatch(x_groups), "etp", axis=1, tiled=True)
    a = jnp.dot(xe, wg, preferred_element_type=F32)
    b = jnp.dot(xe, wu, preferred_element_type=F32)
    dy_own = dispatch(dy_groups)
    own_start, other_start = core * cols, (1 - core) * cols
    if pair:
        dy_other = swap_core(dy_own)
        dy_own, a, b = lax.optimization_barrier((dy_own, a, b))
        raw = jnp.dot(
            dy_own, lax.dynamic_slice_in_dim(wd, own_start, cols, 1).T, preferred_element_type=F32
        ) + jnp.dot(
            dy_other,
            lax.dynamic_slice_in_dim(wd, other_start, cols, 1).T,
            preferred_element_type=F32,
        )
    else:
        dye = lax.all_gather(dy_own, "etp", axis=1, tiled=True)
        raw = jnp.dot(dye, wd.T, preferred_element_type=F32)
    sig = jax.nn.sigmoid(a)
    s = a * sig
    h = s * b
    hs = (gf * h).astype(BF16)
    gate_local = jnp.sum(h * raw, axis=1)
    dh = gf * raw
    da = (dh * b * sig * (1.0 + a * (1.0 - sig))).astype(BF16)
    db = (dh * s).astype(BF16)

    def part(start, width):
        return (
            jnp.dot(
                da, lax.dynamic_slice_in_dim(wg, start, width, 0).T, preferred_element_type=F32
            )
            + jnp.dot(
                db, lax.dynamic_slice_in_dim(wu, start, width, 0).T, preferred_element_type=F32
            )
        ).astype(BF16)

    pieces = 2 if pair else 1
    width = cols // pieces
    grads = []
    last = None
    for i in range(pieces):
        if pair:
            theirs = part(other_start + i * width, width)
            arrived = swap_core(theirs)
            mine = part(own_start + i * width, width)
            last = mine
            share = (mine.astype(F32) + arrived.astype(F32)).astype(BF16)
        else:
            last = part(0, wg.shape[0])
            share = lax.psum_scatter(last, "etp", scatter_dimension=1, tiled=True)
        dense = jnp.einsum(
            "gst,gsc->gtc",
            select,
            share.reshape(groups, per * capacity, width),
            preferred_element_type=F32,
        ).astype(BF16)
        if stepwise:
            grads.append(reduce_planes(dense.reshape(4, 4, rows, width)))
        else:
            grads.append(
                lax.psum_scatter(
                    dense.reshape(ep_count * rows, width), "ep", scatter_dimension=0, tiled=True
                )
            )
    input_grad = jnp.concatenate(grads, axis=1)

    gate_rows = jnp.sum(
        jnp.where(pick, gate_local.reshape(groups, per * capacity, 1), 0.0), axis=1
    ).reshape(ep_count, 1, rows)
    order = blocks[:, None] == jnp.arange(ep_count, dtype=jnp.int32)[None, :]
    gate_rows = jnp.sum(jnp.where(order[:, :, None], gate_rows, 0.0), axis=0)
    gate_rows = lax.psum(gate_rows, "etp")
    gate_back = lax.all_to_all(gate_rows, "ep", split_axis=0, concat_axis=0, tiled=True)
    wanted = expert_ids[:, :, None] == jnp.arange(ep_count, dtype=jnp.int32)[None, None, :]
    gate_grad = jnp.sum(jnp.where(wanted, gate_back.T[:, None, :], 0.0), axis=2)

    hs, da_late, db_late, _ = lax.optimization_barrier((hs, da, db, last))
    if pair:
        first = core == 0
        dye = jnp.concatenate(
            [jnp.where(first, dy_own, dy_other), jnp.where(first, dy_other, dy_own)], axis=1
        )
    gate_weight_gradient = jnp.dot(xe.T, da_late, preferred_element_type=F32).astype(BF16)
    up_weight_gradient = jnp.dot(xe.T, db_late, preferred_element_type=F32).astype(BF16)
    down_weight_gradient = jnp.dot(hs.T, dye, preferred_element_type=F32).astype(BF16)
    return (
        input_grad,
        gate_grad,
        gate_weight_gradient[None],
        up_weight_gradient[None],
        down_weight_gradient[None],
    )


def solution(mesh):
    in_specs = (
        P("ep", "etp"),
        P("ep", "etp"),
        P("ep", None),
        P("ep", None),
        P("ep", None, "etp"),
        P("ep", None, "etp"),
        P("ep", "etp", None),
    )
    out_specs = (
        P("ep", "etp"),
        P("ep", None),
        P("ep", None, "etp"),
        P("ep", None, "etp"),
        P("ep", "etp", None),
    )
    return jax.shard_map(local, mesh=mesh, in_specs=in_specs, out_specs=out_specs, check_vma=False)
```

time: 528 us -> 529 us (level)
  waiting for transfers between devices: 301 us -> 201 us
  local copies, waits for them, and re-layouts: 0.74 us -> 58 us
  starting transfers between devices: 7.97 us -> 57.7 us
  blocking collectives: 34.7 us -> 3.28 us
  other arithmetic: 6.77 us -> 29.4 us
    ppermute x0 -> x47, waiting for transfers between devices: none -> 201 us  [the longest x32 116 us: swap(): return lax.ppermute(value, 'ep', [(i, i ^ bits) for i in range(n)])]
    all_gather x4 -> x1, waiting for transfers between devices: 187 us -> 0.01 us  [local(): xe = lax.all_gather(dispatch(x_groups), 'etp', axis=1, tiled=True)]
    reduce_scatter x2 -> x0, waiting for transfers between devices: 114 us -> none  [the longest x1 95 us: local(): input_grad = lax.psum_scatter(dense, 'ep', scatter_dimension=0, tiled=True)]
    ppermute x0 -> x47, starting transfers between devices: none -> 52.4 us  [the longest x32 34.4 us: swap(): return lax.ppermute(value, 'ep', [(i, i ^ bits) for i in range(n)])]
    unnamed x13 -> x75, local copies, waits for them, and re-layouts: 0.12 us -> 37 us
    all_gather x1 -> x0, blocking collectives: 31.7 us -> none  [local(): routes = lax.all_gather(routes, 'ep', axis=0, tiled=True)]
    slice x0 -> x20, local copies, waits for them, and re-layouts: none -> 13.5 us  [the longest x6 6.76 us: spread_plane(): upper = swap(by_x[:, half:], 2)]
    select_n x0 -> x1, other arithmetic: none -> 7.83 us  [local(): jnp.where(first, dy_own, dy_other)]
  transfers between devices with their start and end apart: 7 -> 49, of which waited for: 5 -> 20; matrix products, arithmetic and copies ran while one was open for 19% -> 39% of each run, Pallas kernels for 0% -> 0%
where the time goes in v2:
time: 529 us; the launch traced here: 522 us
  waiting for transfers between devices  201 us (38%)
  matrix products  158 us (30%)
  local copies, waits for them, and re-layouts  58 us (11%)
  starting transfers between devices  57.7 us (11%)
  other arithmetic  29.4 us (6%)
  between operations  15 us (3%)
    ppermute x32, waiting for transfers between devices, swap(): return lax.ppermute(value, 'ep', [(i, i ^ bits) for i in range(n)])  116 us
    ppermute x12, waiting for transfers between devices, shift(): lax.ppermute(value, 'ep', [(i, (i + 4 * offset) % n) for i in range(n)])  85.1 us
    unnamed x75, local copies, waits for them, and re-layouts  37 us
    ppermute x32, starting transfers between devices, swap(): return lax.ppermute(value, 'ep', [(i, i ^ bits) for i in range(n)])  34.4 us
    dot_general x4, matrix products, part(): jnp.dot(db, lax.dynamic_slice_in_dim(wu, start, width, 0).T, preferred_el...  25.9 us
    dot_general x4, matrix products, part(): jnp.dot(da, lax.dynamic_slice_in_dim(wg, start, width, 0).T, preferred_el...  25.6 us
    dot_general x1, matrix products, local(): jnp.dot(hs.T, dye, preferred_element_type=F32).astype(BF16)  18.9 us
    ppermute x12, starting transfers between devices, shift(): lax.ppermute(value, 'ep', [(i, (i + 4 * offset) % n) for i in range(n)])  17.5 us
  transfers between devices with their start and end apart: 49, of which 20 were waited for; matrix products, arithmetic and copies ran while one was open for 39% of the time, Pallas kernels for 0%

profile of v2, /device:TPU:10, one launch (start us, length us, event | category | flops | bytes accessed | tf_op | source)
XLA Modules:
  0.0 522.5 jit_solution(12173517944383900833)
XLA Ops:
  18.9 16.9 %collective-permute-done.10 = bf16[64,3712]{1,0:T(8,128)(2,1)} collective-permute-done((bf16[64,3712]{1,0:T(8,128)(2,1)S(1)}, bf16[64,3712]{1,0:T(8,128)(2,1)}, u32[]{:S(2)}, u32[]{:S(2)}) %collective-permute-start.10) | collective-permute-done | bytes 475168 | tf_op jit(solution)/shard_map/ppermute | solution.py:17
  36.3 18.3 %collective-permute-done.5 = bf16[64,3712]{1,0:T(8,128)(2,1)S(1)} collective-permute-done((bf16[64,3712]{1,0:T(8,128)(2,1)S(1)}, bf16[64,3712]{1,0:T(8,128)(2,1)S(1)}, u32[]{:S(2)}, u32[]{:S(2)}) %collective-permute-start.5) | collective-permute-done | bytes 475168 | tf_op jit(solution)/shard_map/ppermute | solution.py:17
  68.3 14.2 %collective-permute-done.2 = bf16[1,32,3712]{2,1,0:T(8,128)(2,1)S(1)} collective-permute-done((bf16[1,32,3712]{2,1,0:T(8,128)(2,1)S(1)}, bf16[1,32,3712]{2,1,0:T(8,128)(2,1)S(1)}, u32[]{:S(2)}, u32[]{:S(2)}) %collective-permute-start.2) | collective-permute-done | bytes 237600 | tf_op jit(solution)/shard_map/ppermute | solution.py:22
  83.1 6.3 %collective-permute-done.3 = bf16[1,32,3712]{2,1,0:T(8,128)(2,1)S(1)} collective-permute-done((bf16[1,32,3712]{2,1,0:T(8,128)(2,1)S(1)}, bf16[1,32,3712]{2,1,0:T(8,128)(2,1)S(1)}, u32[]{:S(2)}, u32[]{:S(2)}) %collective-permute-start.3) | collective-permute-done | bytes 237600 | tf_op jit(solution)/shard_map/ppermute | solution.py:22
  98.4 32.1 %collective-permute-done.19 = bf16[64,3584]{1,0:T(8,128)(2,1)S(1)} collective-permute-done((bf16[64,3584]{1,0:T(8,128)(2,1)}, bf16[64,3584]{1,0:T(8,128)(2,1)S(1)}, u32[]{:S(2)}, u32[]{:S(2)}) %collective-permute-start.19) | collective-permute-done | bytes 458784 | tf_op jit(solution)/shard_map/ppermute | solution.py:17
  148.8 20.6 %collective-permute-done.17 = bf16[1,32,3584]{2,1,0:T(8,128)(2,1)S(1)} collective-permute-done((bf16[1,32,3584]{2,1,0:T(8,128)(2,1)S(1)}, bf16[1,32,3584]{2,1,0:T(8,128)(2,1)S(1)}, u32[]{:S(2)}, u32[]{:S(2)}) %collective-permute-start.17) | collective-permute-done | bytes 229408 | tf_op jit(solution)/shard_map/ppermute | solution.py:22
  171.6 4.2 collective-permute-done.13
  178.0 4.4 collective-permute-done.14
  191.6 22.4 %collective-permute-done.8 = bf16[2,32,3712]{2,1,0:T(8,128)(2,1)S(1)} collective-permute-done((bf16[2,32,3712]{2,1,0:T(8,128)(2,1)S(1)}, bf16[2,32,3712]{2,1,0:T(8,128)(2,1)S(1)}, u32[]{:S(2)}, u32[]{:S(2)}) %collective-permute-start.8) | collective-permute-done | bytes 475168 | tf_op jit(solution)/shard_map/ppermute | solution.py:22
  215.2 9.9 %collective-permute-done.9 = bf16[2,32,3712]{2,1,0:T(8,128)(2,1)S(1)} collective-permute-done((bf16[2,32,3712]{2,1,0:T(8,128)(2,1)S(1)}, bf16[2,32,3712]{2,1,0:T(8,128)(2,1)S(1)}, u32[]{:S(2)}, u32[]{:S(2)}) %collective-permute-start.9) | collective-permute-done | bytes 475168 | tf_op jit(solution)/shard_map/ppermute | solution.py:22
  264.2 14.4 %fusion = f32[640,1024]{1,0:T(8,128)S(1)} fusion(bf16[640,7168]{1,0:T(8,128)(2,1)} %all-gather.2.cloned.1.call-done, bf16[1,7168,1024]{2,1,0:T(8,128)(2,1)} %param.13), kind=kOutput, calls=%fused_computation | convolution fusion | flops 9395240960 | bytes 26476544 | tf_op jit(solution)/shard_map/dot_general | solution.py:151
  278.6 13.0 %fusion.2 = f32[640,1024]{1,0:T(8,128)S(1)} fusion(bf16[640,7168]{1,0:T(8,128)(2,1)S(1)} %copy-done.18, bf16[1,7168,1024]{2,1,0:T(8,128)(2,1)} %param.12), kind=kOutput, calls=%fused_computation.2 | convolution fusion | flops 9395240960 | bytes 26476544 | tf_op jit(solution)/shard_map/dot_general | solution.py:150
  291.6 9.9 %fusion.9 = f32[640,1024]{1,0:T(8,128)S(1)} fusion(bf16[640,3584]{1,0:T(8,128)(2,1)} %pad_maximum_fusion, bf16[1,1024,7168]{2,1,0:T(8,128)(2,1)} %param.14, s32[]{:T(128)S(6)} %select_n.90), kind=kOutput, calls=%fused_computation.12 | convolution fusion | flops 4697620480 | bytes 14548996 | tf_op jit(solution)/shard_map/dot_general | solution.py:157
  301.6 11.3 %multiply_reduce_fusion = (f32[640]{0:T(1024)S(1)}, f32[640,1024]{1,0:T(8,128)}) fusion(f32[640,1024]{1,0:T(8,128)S(1)} %fusion, f32[640,1024]{1,0:T(8,128)S(1)} %fusion.2, f32[640,1024]{1,0:T(8,128)S(1)} %fusion.9, bf16[640,3584]{1,0:T(8,128)(2,1)} %collective-permute-done.30, bf16[1,1024,7168]{2,1,0:T(8,128)(2,1)} %param.14, s32[]{:T(128)S(6)} %select_n.91), kind=kOutput, calls=%fused_computation.61 | convolution fusion | flops 4702862848 | bytes 22415876 | tf_op jit(solution)/shard_map/dot_general | solution.py:159
  313.4 4.9 multiply_convert_fusion
  318.3 7.2 %fusion.21 = f32[640,1792]{1,0:T(8,128)} fusion(bf16[640,1024]{1,0:T(8,128)(2,1)S(1)} %get-tuple-element.17, bf16[1,7168,1024]{2,1,0:T(8,128)(2,1)} %param.13, s32[]{:T(128)S(6)} %select_n.91), kind=kOutput, calls=%fused_computation.44 | convolution fusion | flops 2348810240 | bytes 9568260 | tf_op jit(solution)/shard_map/dot_general | solution.py:181
  325.5 6.8 %fusion.25 = f32[640,1792]{1,0:T(8,128)} fusion(bf16[640,1024]{1,0:T(8,128)(2,1)S(1)} %get-tuple-element.17, bf16[1,7168,1024]{2,1,0:T(8,128)(2,1)} %param.13, s32[]{:T(128)S(6)} %select_n.90), kind=kOutput, calls=%fused_computation.48 | convolution fusion | flops 2348810240 | bytes 9568260 | tf_op jit(solution)/shard_map/dot_general | solution.py:181
  335.7 5.2 %all-to-all-start = ((f32[16,1,64]{2,1,0:T(1,128)}), f32[16,1,64]{2,1,0:T(1,128)S(1)}, u32[]{:S(2)}, u32[]{:S(2)}) async-start(f32[16,1,64]{2,1,0:T(1,128)} %bitcast.83), calls=%async_computation | async-start | bytes 16384 | tf_op jit(solution)/shard_map/all_to_all | solution.py:222
  341.0 5.2 fusion.13
  346.2 6.2 %add_convert_fusion.1 = bf16[640,1792]{1,0:T(8,128)(2,1)} fusion(f32[640,1792]{1,0:T(8,128)S(1)} %fusion.13, bf16[640,1024]{1,0:T(8,128)(2,1)S(1)} %copy-done.13, bf16[1,7168,1024]{2,1,0:T(8,128)(2,1)} %param.12, s32[]{:T(128)S(6)} %select_n.93), kind=kOutput, calls=%fused_computation.27 | convolution fusion | flops 2351104000 | bytes 11862020 | tf_op jit(solution)/shard_map/dot_general | solution.py:178
  352.4 6.1 %add_convert_fusion.4 = bf16[640,1792]{1,0:T(8,128)(2,1)} fusion(f32[640,1792]{1,0:T(8,128)S(1)} %bitcast.325, bf16[640,1024]{1,0:T(8,128)(2,1)S(1)} %copy-done.13, bf16[1,7168,1024]{2,1,0:T(8,128)(2,1)} %param.12, s32[]{:T(128)S(6)} %select_n.91), kind=kOutput, calls=%fused_computation.30 | convolution fusion | flops 2351104000 | bytes 11862020 | tf_op jit(solution)/shard_map/dot_general | solution.py:178
  359.0 7.8 %broadcast_select_fusion.1 = (bf16[640,3584]{1,0:T(8,128)(2,1)}, bf16[640,3584]{1,0:T(8,128)(2,1)}) fusion(bf16[640,3584]{1,0:T(8,128)(2,1)} %pad_maximum_fusion, bf16[640,3584]{1,0:T(8,128)(2,1)} %collective-permute-done.30, pred[]{:T(512)S(6)} %eq.69), kind=kLoop, calls=%fused_computation.33 | loop fusion | flops 4587520 | bytes 18350080 | tf_op jit(solution)/shard_map/jit(_where)/select_n | solution.py:230
  366.9 6.8 %fusion.17 = f32[640,1792]{1,0:T(8,128)} fusion(bf16[640,1024]{1,0:T(8,128)(2,1)S(1)} %copy-done.11, bf16[1,7168,1024]{2,1,0:T(8,128)(2,1)} %param.13, s32[]{:T(128)S(6)} %select_n.92), kind=kOutput, calls=%fused_computation.40 | convolution fusion | flops 2348810240 | bytes 9568260 | tf_op jit(solution)/shard_map/dot_general | solution.py:181
  374.3 6.6 %add_convert_fusion = bf16[640,1792]{1,0:T(8,128)(2,1)S(1)} fusion(bf16[640,1792]{1,0:T(8,128)(2,1)} %collective-permute-done.39, f32[640,1792]{1,0:T(8,128)} %fusion.17, bf16[640,1024]{1,0:T(8,128)(2,1)S(1)} %copy-done.13, bf16[1,7168,1024]{2,1,0:T(8,128)(2,1)} %param.12, s32[]{:T(128)S(6)} %select_n.92), kind=kOutput, calls=%fused_computation.26 | convolution fusion | flops 2355691520 | bytes 14155780 | tf_op jit(solution)/shard_map/dot_general | solution.py:178
  387.3 6.6 %add_convert_fusion.3 = bf16[640,1792]{1,0:T(8,128)(2,1)S(1)} fusion(bf16[640,1792]{1,0:T(8,128)(2,1)} %collective-permute-done.31, f32[640,1792]{1,0:T(8,128)} %fusion.25, bf16[640,1024]{1,0:T(8,128)(2,1)S(1)} %copy-done.13, bf16[1,7168,1024]{2,1,0:T(8,128)(2,1)} %param.12, s32[]{:T(128)S(6)} %select_n.90), kind=kOutput, calls=%fused_computation.29 | convolution fusion | flops 2355691520 | bytes 14155780 | tf_op jit(solution)/shard_map/dot_general | solution.py:178
  400.4 14.3 %convert_bitcast_fusion.2 = bf16[1,7168,1024]{2,1,0:T(8,128)(2,1)} fusion(bf16[640,7168]{1,0:T(8,128)(2,1)S(1)} %bitcast.323, bf16[640,1024]{1,0:T(8,128)(2,1)S(1)} %copy-done.13), kind=kOutput, calls=%fused_computation.6 | convolution fusion | flops 9402580992 | bytes 25165824 | tf_op jit(solution)/shard_map/dot_general | solution.py:232
  414.7 14.3 %convert_bitcast_fusion.1 = bf16[1,7168,1024]{2,1,0:T(8,128)(2,1)} fusion(bf16[640,7168]{1,0:T(8,128)(2,1)S(1)} %bitcast.323, bf16[640,1024]{1,0:T(8,128)(2,1)S(1)} %copy-done.12), kind=kOutput, calls=%fused_computation.5 | convolution fusion | flops 9402580992 | bytes 25165824 | tf_op jit(solution)/shard_map/dot_general | solution.py:233
  428.9 18.9 %convert_bitcast_fusion = bf16[1,1024,7168]{2,1,0:T(8,128)(2,1)} fusion(bf16[640,1024]{1,0:T(8,128)(2,1)S(1)} %copy-done.9, bf16[640,3584]{1,0:T(8,128)(2,1)} %get-tuple-element.24, bf16[640,3584]{1,0:T(8,128)(2,1)} %get-tuple-element.23), kind=kOutput, calls=%fused_computation.4 | convolution fusion | flops 9420931072 | bytes 25165824 | tf_op jit(solution)/shard_map/dot_general | solution.py:234
  455.5 17.4 %collective-permute-done.43 = bf16[4,64,1792]{2,1,0:T(8,128)(2,1)S(1)} collective-permute-done((bf16[4,64,1792]{2,1,0:T(8,128)(2,1)S(1)}, bf16[4,64,1792]{2,1,0:T(8,128)(2,1)S(1)}, u32[]{:S(2)}, u32[]{:S(2)}) %collective-permute-start.43) | collective-permute-done | bytes 917536 | tf_op jit(solution)/shard_map/ppermute | solution.py:22
  480.2 10.2 %collective-permute-done.35 = bf16[4,64,1792]{2,1,0:T(8,128)(2,1)S(1)} collective-permute-done((bf16[4,64,1792]{2,1,0:T(8,128)(2,1)S(1)}, bf16[4,64,1792]{2,1,0:T(8,128)(2,1)S(1)}, u32[]{:S(2)}, u32[]{:S(2)}) %collective-permute-start.35) | collective-permute-done | bytes 917536 | tf_op jit(solution)/shard_map/ppermute | solution.py:22
  496.4 7.7 %collective-permute-done.45 = bf16[64,1792]{1,0:T(8,128)(2,1)S(1)} collective-permute-done((bf16[64,1792]{1,0:T(8,128)(2,1)S(1)}, bf16[64,1792]{1,0:T(8,128)(2,1)S(1)}, u32[]{:S(2)}, u32[]{:S(2)}) %collective-permute-start.45) | collective-permute-done | bytes 229408 | tf_op jit(solution)/shard_map/ppermute | solution.py:17
  504.2 4.6 collective-permute-done.36
  (246 shorter events, 152.7 us)
Async XLA Ops:
  7.2 257.0 %all-gather.2.cloned.1.call-start = ((), (), s32[]{:S(2)}) async-start(), calls=%async_computation.1 | async-start | bytes 13762560 | tf_op jit(solution)/shard_map/all_gather | solution.py:149
  9.9 49.4 %collective-permute-start.1 = (bf16[1,64,3712]{2,1,0:T(8,128)(2,1)S(1)}, bf16[1,64,3712]{2,1,0:T(8,128)(2,1)}, u32[]{:S(2)}, u32[]{:S(2)}) collective-permute-start(bf16[1,64,3712]{2,1,0:T(8,128)(2,1)S(1)} %bitcast.314), channel_id=1, source_target_pairs={{0,4},{2,6},{4,0},{6,2},{8,12},{10,14},{12,8},{14,10},{16,20},{18,... | collective-permute-start | bytes 1425416 | tf_op jit(solution)/shard_map/ppermute | solution.py:22
  11.5 50.4 %collective-permute-start = (bf16[1,64,3712]{2,1,0:T(8,128)(2,1)S(1)}, bf16[1,64,3712]{2,1,0:T(8,128)(2,1)}, u32[]{:S(2)}, u32[]{:S(2)}) collective-permute-start(bf16[1,64,3712]{2,1,0:T(8,128)(2,1)S(1)} %bitcast.315), channel_id=1, source_target_pairs={{0,2},{2,0},{4,6},{6,4},{8,10},{10,8},{12,14},{14,12},{16,18},{18,... | collective-permute-start | bytes 1425416 | tf_op jit(solution)/shard_map/ppermute | solution.py:22
  12.0 23.8 %collective-permute-start.10 = (bf16[64,3712]{1,0:T(8,128)(2,1)S(1)}, bf16[64,3712]{1,0:T(8,128)(2,1)}, u32[]{:S(2)}, u32[]{:S(2)}) collective-permute-start(bf16[64,3712]{1,0:T(8,128)(2,1)S(1)} %concatenate.54), channel_id=1, source_target_pairs={{0,16},{2,18},{4,20},{6,22},{8,24},{10,26},{12,28},{14,30},{16,0},... | collective-permute-start | bytes 1425416 | tf_op jit(solution)/shard_map/ppermute | solution.py:17
  14.6 40.0 %collective-permute-start.5 = (bf16[64,3712]{1,0:T(8,128)(2,1)S(1)}, bf16[64,3712]{1,0:T(8,128)(2,1)S(1)}, u32[]{:S(2)}, u32[]{:S(2)}) collective-permute-start(bf16[64,3712]{1,0:T(8,128)(2,1)S(1)} %concatenate.54), channel_id=1, source_target_pairs={{0,8},{2,10},{4,12},{6,14},{8,16},{10,18},{12,20},{14,22},{16,24},... | collective-permute-start | bytes 1425416 | tf_op jit(solution)/shard_map/ppermute | solution.py:17
  14.6 41.5 %collective-permute-start.4 = (bf16[64,3712]{1,0:T(8,128)(2,1)S(1)}, bf16[64,3712]{1,0:T(8,128)(2,1)S(1)}, u32[]{:S(2)}, u32[]{:S(2)}) collective-permute-start(bf16[64,3712]{1,0:T(8,128)(2,1)S(1)} %concatenate.54), channel_id=1, source_target_pairs={{0,24},{2,26},{4,28},{6,30},{8,0},{10,2},{12,4},{14,6},{16,8},{18,... | collective-permute-start | bytes 1425416 | tf_op jit(solution)/shard_map/ppermute | solution.py:17
  35.8 107.8 %collective-permute-start.12 = (bf16[1,64,3712]{2,1,0:T(8,128)(2,1)}, bf16[1,64,3712]{2,1,0:T(8,128)(2,1)}, u32[]{:S(2)}, u32[]{:S(2)}) collective-permute-start(bf16[1,64,3712]{2,1,0:T(8,128)(2,1)} %bitcast.15), channel_id=1, source_target_pairs={{0,4},{2,6},{4,0},{6,2},{8,12},{10,14},{12,8},{14,10},{16,20},{18,... | collective-permute-start | bytes 1425416 | tf_op jit(solution)/shard_map/ppermute | solution.py:22
  54.6 86.6 %collective-permute-start.11 = (bf16[1,64,3712]{2,1,0:T(8,128)(2,1)}, bf16[1,64,3712]{2,1,0:T(8,128)(2,1)}, u32[]{:S(2)}, u32[]{:S(2)}) collective-permute-start(bf16[1,64,3712]{2,1,0:T(8,128)(2,1)} %bitcast.15), channel_id=1, source_target_pairs={{0,2},{2,0},{4,6},{6,4},{8,10},{10,8},{12,14},{14,12},{16,18},{18,... | collective-permute-start | bytes 1425416 | tf_op jit(solution)/shard_map/ppermute | solution.py:22
  58.0 37.2 %collective-permute-start.16 = (bf16[1,64,3584]{2,1,0:T(8,128)(2,1)}, bf16[1,64,3584]{2,1,0:T(8,128)(2,1)}, u32[]{:S(2)}, u32[]{:S(2)}) collective-permute-start(bf16[1,64,3584]{2,1,0:T(8,128)(2,1)} %bitcast.21), channel_id=1, source_target_pairs={{0,4},{2,6},{4,0},{6,2},{8,12},{10,14},{12,8},{14,10},{16,20},{18,... | collective-permute-start | bytes 1376264 | tf_op jit(solution)/shard_map/ppermute | solution.py:22
  59.3 31.5 %collective-permute-start.15 = (bf16[1,64,3584]{2,1,0:T(8,128)(2,1)}, bf16[1,64,3584]{2,1,0:T(8,128)(2,1)}, u32[]{:S(2)}, u32[]{:S(2)}) collective-permute-start(bf16[1,64,3584]{2,1,0:T(8,128)(2,1)} %bitcast.21), channel_id=1, source_target_pairs={{0,2},{2,0},{4,6},{6,4},{8,10},{10,8},{12,14},{14,12},{16,18},{18,... | collective-permute-start | bytes 1376264 | tf_op jit(solution)/shard_map/ppermute | solution.py:22
  89.4 42.5 %collective-permute-start.25 = (bf16[64,3584]{1,0:T(8,128)(2,1)}, bf16[64,3584]{1,0:T(8,128)(2,1)}, u32[]{:S(2)}, u32[]{:S(2)}) collective-permute-start(bf16[64,3584]{1,0:T(8,128)(2,1)} %param.9), channel_id=1, source_target_pairs={{0,16},{2,18},{4,20},{6,22},{8,24},{10,26},{12,28},{14,30},{16,0},... | collective-permute-start | bytes 1376264 | tf_op jit(solution)/shard_map/ppermute | solution.py:17
  90.8 44.5 %collective-permute-start.20 = (bf16[64,3584]{1,0:T(8,128)(2,1)}, bf16[64,3584]{1,0:T(8,128)(2,1)S(1)}, u32[]{:S(2)}, u32[]{:S(2)}) collective-permute-start(bf16[64,3584]{1,0:T(8,128)(2,1)} %param.9), channel_id=1, source_target_pairs={{0,8},{2,10},{4,12},{6,14},{8,16},{10,18},{12,20},{14,22},{16,24},... | collective-permute-start | bytes 1376264 | tf_op jit(solution)/shard_map/ppermute | solution.py:17
  95.1 35.4 %collective-permute-start.19 = (bf16[64,3584]{1,0:T(8,128)(2,1)}, bf16[64,3584]{1,0:T(8,128)(2,1)S(1)}, u32[]{:S(2)}, u32[]{:S(2)}) collective-permute-start(bf16[64,3584]{1,0:T(8,128)(2,1)} %param.9), channel_id=1, source_target_pairs={{0,24},{2,26},{4,28},{6,30},{8,0},{10,2},{12,4},{14,6},{16,8},{18,... | collective-permute-start | bytes 1376264 | tf_op jit(solution)/shard_map/ppermute | solution.py:17
  130.6 55.0 %collective-permute-start.7 = (bf16[2,64,3712]{2,1,0:T(8,128)(2,1)}, bf16[2,64,3712]{2,1,0:T(8,128)(2,1)S(1)}, u32[]{:S(2)}, u32[]{:S(2)}) collective-permute-start(bf16[2,64,3712]{2,1,0:T(8,128)(2,1)} %pad_maximum_fusion.2), channel_id=1, source_target_pairs={{0,4},{2,6},{4,0},{6,2},{8,12},{10,14},{12,8},{14,10},{16,20},{18,... | collective-permute-start | bytes 2850824 | tf_op jit(solution)/shard_map/ppermute | solution.py:22
  131.9 55.2 %collective-permute-start.6 = (bf16[2,64,3712]{2,1,0:T(8,128)(2,1)}, bf16[2,64,3712]{2,1,0:T(8,128)(2,1)}, u32[]{:S(2)}, u32[]{:S(2)}) collective-permute-start(bf16[2,64,3712]{2,1,0:T(8,128)(2,1)} %pad_maximum_fusion.2), channel_id=1, source_target_pairs={{0,2},{2,0},{4,6},{6,4},{8,10},{10,8},{12,14},{14,12},{16,18},{18,... | collective-permute-start | bytes 2850824 | tf_op jit(solution)/shard_map/ppermute | solution.py:22
  135.2 100.5 %collective-permute-start.27 = (bf16[1,64,3584]{2,1,0:T(8,128)(2,1)}, bf16[1,64,3584]{2,1,0:T(8,128)(2,1)S(1)}, u32[]{:S(2)}, u32[]{:S(2)}) collective-permute-start(bf16[1,64,3584]{2,1,0:T(8,128)(2,1)} %bitcast.39), channel_id=1, source_target_pairs={{0,4},{2,6},{4,0},{6,2},{8,12},{10,14},{12,8},{14,10},{16,20},{18,... | collective-permute-start | bytes 1376264 | tf_op jit(solution)/shard_map/ppermute | solution.py:22
  141.2 96.1 %collective-permute-start.26 = (bf16[1,64,3584]{2,1,0:T(8,128)(2,1)}, bf16[1,64,3584]{2,1,0:T(8,128)(2,1)}, u32[]{:S(2)}, u32[]{:S(2)}) collective-permute-start(bf16[1,64,3584]{2,1,0:T(8,128)(2,1)} %bitcast.39), channel_id=1, source_target_pairs={{0,2},{2,0},{4,6},{6,4},{8,10},{10,8},{12,14},{14,12},{16,18},{18,... | collective-permute-start | bytes 1376264 | tf_op jit(solution)/shard_map/ppermute | solution.py:22
  143.6 25.8 %collective-permute-start.17 = (bf16[1,32,3584]{2,1,0:T(8,128)(2,1)S(1)}, bf16[1,32,3584]{2,1,0:T(8,128)(2,1)S(1)}, u32[]{:S(2)}, u32[]{:S(2)}) collective-permute-start(bf16[1,32,3584]{2,1,0:T(8,128)(2,1)S(1)} %slice.281), channel_id=1, source_target_pairs={{0,2},{2,0},{4,6},{6,4},{8,10},{10,8},{12,14},{14,12},{16,18},{18,... | collective-permute-start | bytes 688136 | tf_op jit(solution)/shard_map/ppermute | solution.py:22
  182.4 65.2 %collective-permute-start.22 = (bf16[2,64,3584]{2,1,0:T(8,128)(2,1)}, bf16[2,64,3584]{2,1,0:T(8,128)(2,1)}, u32[]{:S(2)}, u32[]{:S(2)}) collective-permute-start(bf16[2,64,3584]{2,1,0:T(8,128)(2,1)} %pad_maximum_fusion.3), channel_id=1, source_target_pairs={{0,4},{2,6},{4,0},{6,2},{8,12},{10,14},{12,8},{14,10},{16,20},{18,... | collective-permute-start | bytes 2752520 | tf_op jit(solution)/shard_map/ppermute | solution.py:22
  185.5 64.4 %collective-permute-start.21 = (bf16[2,64,3584]{2,1,0:T(8,128)(2,1)}, bf16[2,64,3584]{2,1,0:T(8,128)(2,1)}, u32[]{:S(2)}, u32[]{:S(2)}) collective-permute-start(bf16[2,64,3584]{2,1,0:T(8,128)(2,1)} %pad_maximum_fusion.3), channel_id=1, source_target_pairs={{0,2},{2,0},{4,6},{6,4},{8,10},{10,8},{12,14},{14,12},{16,18},{18,... | collective-permute-start | bytes 2752520 | tf_op jit(solution)/shard_map/ppermute | solution.py:22
  187.1 26.9 %collective-permute-start.8 = (bf16[2,32,3712]{2,1,0:T(8,128)(2,1)S(1)}, bf16[2,32,3712]{2,1,0:T(8,128)(2,1)S(1)}, u32[]{:S(2)}, u32[]{:S(2)}) collective-permute-start(bf16[2,32,3712]{2,1,0:T(8,128)(2,1)S(1)} %slice.265), channel_id=1, source_target_pairs={{0,2},{2,0},{4,6},{6,4},{8,10},{10,8},{12,14},{14,12},{16,18},{18,... | collective-permute-start | bytes 1425416 | tf_op jit(solution)/shard_map/ppermute | solution.py:22
  264.2 37.4 %collective-permute-start.30 = (bf16[640,3584]{1,0:T(8,128)(2,1)}, bf16[640,3584]{1,0:T(8,128)(2,1)}, u32[]{:S(2)}, u32[]{:S(2)}) collective-permute-start(bf16[640,3584]{1,0:T(8,128)(2,1)} %pad_maximum_fusion), channel_id=1, source_target_pairs={{0,1},{1,0},{2,3},{3,2},{4,5},{5,4},{6,7},{7,6},{8,9},{9,8},{10,11... | collective-permute-start | bytes 13762568 | tf_op jit(solution)/shard_map/ppermute | solution.py:26
  335.7 37.9 %all-to-all-start = ((f32[16,1,64]{2,1,0:T(1,128)}), f32[16,1,64]{2,1,0:T(1,128)S(1)}, u32[]{:S(2)}, u32[]{:S(2)}) async-start(f32[16,1,64]{2,1,0:T(1,128)} %bitcast.83), calls=%async_computation | async-start | bytes 16384 | tf_op jit(solution)/shard_map/all_to_all | solution.py:222
  358.5 28.7 %collective-permute-start.31 = (bf16[640,1792]{1,0:T(8,128)(2,1)}, bf16[640,1792]{1,0:T(8,128)(2,1)}, u32[]{:S(2)}, u32[]{:S(2)}) collective-permute-start(bf16[640,1792]{1,0:T(8,128)(2,1)} %add_convert_fusion.4), channel_id=1, source_target_pairs={{0,1},{1,0},{2,3},{3,2},{4,5},{5,4},{6,7},{7,6},{8,9},{9,8},{10,11... | collective-permute-start | bytes 6881288 | tf_op jit(solution)/shard_map/ppermute | solution.py:26
  385.0 62.8 %collective-permute-start.42 = (bf16[4,32,1792]{2,1,0:T(8,128)(2,1)}, bf16[4,32,1792]{2,1,0:T(8,128)(2,1)}, u32[]{:S(2)}, u32[]{:S(2)}) collective-permute-start(bf16[4,32,1792]{2,1,0:T(8,128)(2,1)} %get-tuple-element.35), channel_id=1, source_target_pairs={{0,2},{2,0},{4,6},{6,4},{8,10},{10,8},{12,14},{14,12},{16,18},{18,... | collective-permute-start | bytes 1376264 | tf_op jit(solution)/shard_map/ppermute | solution.py:22
  385.6 62.3 %collective-permute-start.40 = (bf16[4,32,1792]{2,1,0:T(8,128)(2,1)}, bf16[4,32,1792]{2,1,0:T(8,128)(2,1)}, u32[]{:S(2)}, u32[]{:S(2)}) collective-permute-start(bf16[4,32,1792]{2,1,0:T(8,128)(2,1)} %get-tuple-element.36), channel_id=1, source_target_pairs={{0,4},{2,6},{4,0},{6,2},{8,12},{10,14},{12,8},{14,10},{16,20},{18,... | collective-permute-start | bytes 1376264 | tf_op jit(solution)/shard_map/ppermute | solution.py:22
  398.0 53.4 %collective-permute-start.34 = (bf16[4,32,1792]{2,1,0:T(8,128)(2,1)}, bf16[4,32,1792]{2,1,0:T(8,128)(2,1)}, u32[]{:S(2)}, u32[]{:S(2)}) collective-permute-start(bf16[4,32,1792]{2,1,0:T(8,128)(2,1)} %get-tuple-element.29), channel_id=1, source_target_pairs={{0,2},{2,0},{4,6},{6,4},{8,10},{10,8},{12,14},{14,12},{16,18},{18,... | collective-permute-start | bytes 1376264 | tf_op jit(solution)/shard_map/ppermute | solution.py:22
  399.5 52.0 %collective-permute-start.32 = (bf16[4,32,1792]{2,1,0:T(8,128)(2,1)}, bf16[4,32,1792]{2,1,0:T(8,128)(2,1)}, u32[]{:S(2)}, u32[]{:S(2)}) collective-permute-start(bf16[4,32,1792]{2,1,0:T(8,128)(2,1)} %get-tuple-element.30), channel_id=1, source_target_pairs={{0,4},{2,6},{4,0},{6,2},{8,12},{10,14},{12,8},{14,10},{16,20},{18,... | collective-permute-start | bytes 1376264 | tf_op jit(solution)/shard_map/ppermute | solution.py:22
  450.8 23.4 %collective-permute-start.41 = (bf16[4,64,1792]{2,1,0:T(8,128)(2,1)S(1)}, bf16[4,64,1792]{2,1,0:T(8,128)(2,1)S(1)}, u32[]{:S(2)}, u32[]{:S(2)}) collective-permute-start(bf16[4,64,1792]{2,1,0:T(8,128)(2,1)S(1)} %pad_maximum_fusion.6), channel_id=1, source_target_pairs={{0,2},{2,0},{4,6},{6,4},{8,10},{10,8},{12,14},{14,12},{16,18},{18,... | collective-permute-start | bytes 2752520 | tf_op jit(solution)/shard_map/ppermute | solution.py:22
  453.0 37.4 %collective-permute-start.35 = (bf16[4,64,1792]{2,1,0:T(8,128)(2,1)S(1)}, bf16[4,64,1792]{2,1,0:T(8,128)(2,1)S(1)}, u32[]{:S(2)}, u32[]{:S(2)}) collective-permute-start(bf16[4,64,1792]{2,1,0:T(8,128)(2,1)S(1)} %pad_maximum_fusion.5), channel_id=1, source_target_pairs={{0,4},{2,6},{4,0},{6,2},{8,12},{10,14},{12,8},{14,10},{16,20},{18,... | collective-permute-start | bytes 2752520 | tf_op jit(solution)/shard_map/ppermute | solution.py:22
  454.2 37.4 %collective-permute-start.33 = (bf16[4,64,1792]{2,1,0:T(8,128)(2,1)S(1)}, bf16[4,64,1792]{2,1,0:T(8,128)(2,1)S(1)}, u32[]{:S(2)}, u32[]{:S(2)}) collective-permute-start(bf16[4,64,1792]{2,1,0:T(8,128)(2,1)S(1)} %pad_maximum_fusion.4), channel_id=1, source_target_pairs={{0,2},{2,0},{4,6},{6,4},{8,10},{10,8},{12,14},{14,12},{16,18},{18,... | collective-permute-start | bytes 2752520 | tf_op jit(solution)/shard_map/ppermute | solution.py:22
  478.7 25.4 %collective-permute-start.45 = (bf16[64,1792]{1,0:T(8,128)(2,1)S(1)}, bf16[64,1792]{1,0:T(8,128)(2,1)S(1)}, u32[]{:S(2)}, u32[]{:S(2)}) collective-permute-start(bf16[64,1792]{1,0:T(8,128)(2,1)S(1)} %get-tuple-element.49), channel_id=1, source_target_pairs={{0,24},{2,26},{4,28},{6,30},{8,0},{10,2},{12,4},{14,6},{16,8},{18,... | collective-permute-start | bytes 688136 | tf_op jit(solution)/shard_map/ppermute | solution.py:17
  (41 other events, 487.7 us)
Sparse Core Ops, SparseCore 0:
  235.2 20.9 all-gather.1
